TPU v7x, 32 devices: a whole 2x2x4 slice. The times are simulated.
32 devices in a mesh: groups: 2 (over y), dev: 4 (over z), pd: 4 (over x, core).
Axes of the slice: x: 2, y: 2, z: 4, core: 2. Of those that a mesh axis runs over, the one named last changes fastest.
Arguments:
- queries: bfloat16 [64, 4, 16, 192], P(('groups', 'dev', 'pd')), parts along dimension 0, may hold values from -250 to 250
- new_latents: bfloat16 [64, 4, 576], P(('groups', 'dev', 'pd')), parts along dimension 0, may hold values from -4 to 4
- prompt_blocks: bfloat16 [512, 128, 576], P(('groups', 'dev', 'pd')), parts along dimension 0, may hold values from -6 to 6
- block_routes: int32 [512, 3], P(('groups', 'dev', 'pd')), parts along dimension 0, may hold values from 0 to 31, as said below
- prompt_lengths: int32 [64], P(('groups', 'dev', 'pd')), parts along dimension 0, may hold values from 0 to 4096, as said below
- resident_blocks: bfloat16 [512, 128, 576], P(('groups', 'dev', 'pd')), parts along dimension 0, may hold values from -6 to 6
- resident_slots: int32 [512], P(('groups', 'dev', 'pd')), parts along dimension 0, may hold values from 0 to 1
- key_absorb: bfloat16 [16, 128, 512], P('dev'), may hold values from -0.5 to 0.5
- value_expand: bfloat16 [16, 512, 128], P('dev'), may hold values from -6 to 6
- output_weight: bfloat16 [2048, 7168], P('dev'), may hold values from -0.125 to 0.125
Outputs:
- mixed: bfloat16 [256, 7168], P(('groups', 'dev', 'pd')), parts along dimension 0
There are 2 independent parts, one for each index of `groups`. A program takes and returns all parts, laid end to end along the dimension named above; an argument that names none is the same for every part. Nothing has to cross between parts.
Inputs may be any that keep to these rules, and one draw needn't show every extreme that they name: block_routes[b] = (destination dev index in the holder's pd row, request slot below 2, position of the block in its request's prompt). At most 8 blocks of one device go to one destination, and in every pd row some device receives exactly 8 blocks from every device. The positions of one request's blocks are 0, 1, 2, ... without gaps, in order of holder. `prompt_lengths`: a request with k prompt blocks has a length of 128 * (k - 1) + 1 to 128 * k, and 0 when k = 0.
All inputs are finite; a program needn't handle non-finite values.
Results may differ from a plain program's by a relative error of at most 0.017.
Values may be sent and summed in bfloat16 or wider, within the bound.
A program may use at most 128 MiB of HBM per device.

v0:
```python
import math

import jax
import jax.numpy as jnp
from jax import lax
from jax.sharding import PartitionSpec as P

KVR = 512


def deliver(prompt_blocks, block_routes, prompt_lengths):
    devices = lax.axis_size("dev")
    held = prompt_blocks.shape[0]
    width = prompt_blocks.shape[1]
    per_pair = max(1, 2 * held // devices)
    places = devices * per_pair
    destination = block_routes[:, 0]
    mine = (destination[:, None] == jnp.arange(devices, dtype=jnp.int32)[None, :]).astype(jnp.int32)
    rank = jnp.sum((jnp.cumsum(mine, axis=0) - mine) * mine, axis=1)
    position = destination * per_pair + rank
    select = jnp.arange(places, dtype=jnp.int32)[:, None] == position[None, :]
    outgoing = jnp.einsum(
        "sp,pbc->sbc",
        select.astype(jnp.bfloat16),
        prompt_blocks,
        preferred_element_type=jnp.float32,
    ).astype(jnp.bfloat16)
    marks = jnp.concatenate([jnp.ones((held, 1), jnp.int32), block_routes[:, 1:3]], axis=1)
    labels = jnp.sum(select.astype(jnp.int32)[:, :, None] * marks[None, :, :], axis=1)
    arrived, tags = (
        lax.all_to_all(
            outgoing.reshape(devices, per_pair, width, -1),
            "dev",
            split_axis=0,
            concat_axis=0,
            tiled=True,
        ),
        lax.all_to_all(
            labels.reshape(devices, per_pair, 3), "dev", split_axis=0, concat_axis=0, tiled=True
        ),
    )
    arrived = arrived.reshape(places, width, -1)
    tags = tags.reshape(places, 3)
    owners = tags[:, 1]
    requests = prompt_lengths.shape[0]
    lengths = jnp.sum(
        jnp.where(
            owners[:, None] == jnp.arange(requests, dtype=jnp.int32)[None, :],
            prompt_lengths[None, :],
            0,
        ),
        axis=1,
    )
    valid = tags[:, 0] * jnp.clip(lengths - width * tags[:, 2], 0, width)
    return (arrived, owners, valid)


def opening(queries, fresh, heads, scale):
    scores = jnp.einsum("rqc,rkc->rqk", queries, fresh, preferred_element_type=jnp.float32) * scale
    causal = jnp.arange(fresh.shape[1])[None, :] <= (jnp.arange(queries.shape[1]) // heads)[:, None]
    scores = jnp.where(causal[None], scores, -1e30)
    top = jnp.max(scores, axis=2)
    weight = jnp.where(causal[None], jnp.exp(scores - top[..., None]), 0.0)
    total = jnp.sum(weight, axis=2)
    carried = jnp.einsum(
        "rqk,rkc->rqc",
        weight.astype(jnp.bfloat16),
        fresh[..., :KVR],
        preferred_element_type=jnp.float32,
    )
    return (top, total, carried)


def sweep(state, queries, blocks, owners, valid, scale):
    count = blocks.shape[0]
    group = math.gcd(count, 8)
    rounds = count // group
    width = blocks.shape[1]
    requests = queries.shape[0]
    grouped = (
        blocks.reshape(rounds, group, width, blocks.shape[2]),
        owners.reshape(rounds, group),
        valid.reshape(rounds, group),
    )

    def advance(carry, piece):
        top, total, accum = carry
        block_keys, block_owner, block_valid = piece
        picked = jnp.take(queries, block_owner, axis=0)
        scores = (
            jnp.einsum("gqc,gkc->gqk", picked, block_keys, preferred_element_type=jnp.float32)
            * scale
        )
        live = jnp.arange(width)[None, :] < block_valid[:, None]
        scores = jnp.where(live[:, None, :], scores, -1e30)
        owned = block_owner[:, None] == jnp.arange(requests, dtype=jnp.int32)[None, :]
        best = jnp.max(
            jnp.where(owned[:, :, None], jnp.max(scores, axis=2)[:, None, :], -1e30), axis=0
        )
        new_top = jnp.maximum(top, best)
        weight = jnp.where(
            live[:, None, :],
            jnp.exp(scores - jnp.take(new_top, block_owner, axis=0)[:, :, None]),
            0.0,
        )
        ownf = owned.astype(jnp.float32)
        mass = jnp.einsum("gr,gq->rq", ownf, jnp.sum(weight, axis=2))
        carried = jnp.einsum(
            "gqk,gkc->gqc",
            weight.astype(jnp.bfloat16),
            block_keys[..., :KVR],
            preferred_element_type=jnp.float32,
        )
        factor = jnp.exp(top - new_top)
        total = total * factor + mass
        accum = accum * factor[..., None] + jnp.einsum("gr,gqc->rqc", ownf, carried)
        return ((new_top, total, accum), None)

    state, unused = lax.scan(advance, state, grouped)
    return state


def shards(
    queries,
    new_latents,
    prompt_blocks,
    block_routes,
    prompt_lengths,
    resident_blocks,
    resident_slots,
    key_absorb,
    value_expand,
    output_weight,
):
    requests = queries.shape[0]
    steps = queries.shape[1]
    split_at = key_absorb.shape[1]
    scale = 1.0 / math.sqrt(queries.shape[3])
    piece = lax.all_to_all(queries, "dev", split_axis=2, concat_axis=0, tiled=True)
    latent = jnp.einsum(
        "rshn,hnc->rshc", piece[..., :split_at], key_absorb, preferred_element_type=jnp.float32
    ).astype(jnp.bfloat16)
    joined = jnp.concatenate([latent, piece[..., split_at:]], axis=-1)
    absorbed = lax.all_to_all(joined, "dev", split_axis=0, concat_axis=2, tiled=True)
    heads = absorbed.shape[2]
    flat_queries = absorbed.reshape(requests, steps * heads, absorbed.shape[3])
    state = opening(flat_queries, new_latents, heads, scale)
    home_valid = jnp.full((resident_blocks.shape[0],), resident_blocks.shape[1], jnp.int32)
    arrived, owners, valid = deliver(prompt_blocks, block_routes, prompt_lengths)
    joined_blocks = jnp.concatenate([resident_blocks, arrived], axis=0)
    joined_owners = jnp.concatenate([resident_slots, owners], axis=0)
    joined_valid = jnp.concatenate([home_valid, valid], axis=0)
    state = sweep(state, flat_queries, joined_blocks, joined_owners, joined_valid, scale)
    top, total, accum = state
    latent_out = (accum / total[..., None]).astype(jnp.bfloat16).reshape(requests, steps, heads, -1)
    expanded = jnp.einsum(
        "rshc,hcv->rshv",
        lax.all_to_all(latent_out, "dev", split_axis=2, concat_axis=0, tiled=True),
        value_expand,
        preferred_element_type=jnp.float32,
    ).astype(jnp.bfloat16)
    flat = expanded.reshape(expanded.shape[0] * steps, -1)
    mixed = lax.psum_scatter(
        jnp.dot(flat, output_weight, preferred_element_type=jnp.float32).astype(jnp.bfloat16),
        "dev",
        scatter_dimension=0,
        tiled=True,
    )
    return mixed


def solution(mesh):
    in_specs = (
        P(("groups", "dev", "pd"), None, None, None),
        P(("groups", "dev", "pd"), None, None),
        P(("groups", "dev", "pd"), None, None),
        P(("groups", "dev", "pd"), None),
        P(("groups", "dev", "pd")),
        P(("groups", "dev", "pd"), None, None),
        P(("groups", "dev", "pd")),
        P("dev", None, None),
        P("dev", None, None),
        P("dev", None),
    )
    out_specs = P(("groups", "dev", "pd"), None)
    return jax.shard_map(shards, mesh=mesh, in_specs=in_specs, out_specs=out_specs, check_vma=False)
```

profile of v0, /device:TPU:0, one launch (start us, length us, event | category | flops | bytes accessed | tf_op | source)
XLA Modules:
  0.0 314.8 jit_solution(4139259342923842031)
XLA Ops:
  8.2 6.3 %all-to-all-start = ((bf16[2,4,16,192]{3,1,0,2:T(4,128)(2,1)}), bf16[2,4,16,192]{3,1,0,2:T(4,128)(2,1)S(1)}, u32[]{:S(2)}, u32[]{:S(2)}) async-start(bf16[2,4,16,192]{3,1,0,2:T(4,128)(2,1)} %copy.77), calls=%async_computation | async-start | bytes 131072 | tf_op jit(solution)/shard_map/all_to_all | solution.py:139
  17.7 2.5 all-to-all-done
  20.3 3.2 %all-to-all-start.2 = ((s32[4,8,3]{1,2,0:T(4,128)}), s32[4,8,3]{1,2,0:T(4,128)S(1)}, u32[]{:S(2)}, u32[]{:S(2)}) async-start(s32[4,8,3]{1,2,0:T(4,128)} %copy.81), calls=%async_computation.2 | async-start | bytes 16384 | tf_op jit(solution)/shard_map/all_to_all | solution.py:38
  25.7 3.4 %all-to-all-done.2 = s32[4,8,3]{1,2,0:T(4,128)S(1)} async-done(((s32[4,8,3]{1,2,0:T(4,128)}), s32[4,8,3]{1,2,0:T(4,128)S(1)}, u32[]{:S(2)}, u32[]{:S(2)}) %all-to-all-start.2) | async-done | bytes 416 | tf_op jit(solution)/shard_map/all_to_all | solution.py:38
  29.1 3.3 %all-to-all-start.1 = ((bf16[8,4,4,576]{3,1,2,0:T(4,128)(2,1)}), bf16[8,4,4,576]{3,1,2,0:T(4,128)(2,1)S(1)}, u32[]{:S(2)}, u32[]{:S(2)}) async-start(bf16[8,4,4,576]{3,1,2,0:T(4,128)(2,1)} %copy.79), calls=%async_computation.1 | async-start | bytes 327680 | tf_op jit(solution)/shard_map/all_to_all | solution.py:144
  32.4 5.5 %convert_bitcast_fusion = bf16[4,8,128,576]{2,1,0,3:T(8,128)(2,1)S(1)} fusion(bf16[16,128,576]{1,2,0:T(8,128)(2,1)S(1)} %copy-done, s32[16]{0:T(128)S(1)} %multiply_add_fusion), kind=kOutput, calls=%fused_computation.38 | convolution fusion | flops 77857280 | bytes 7077952 | tf_op jit(solution)/shard_map/sp,pbc->sbc/dot_general | solution.py:22
  38.0 2.9 copy.84
  40.9 5.2 %all-to-all-start.3 = ((bf16[4,8,128,576]{2,1,3,0:T(8,128)(2,1)}), bf16[4,8,128,576]{2,1,3,0:T(8,128)(2,1)}, u32[]{:S(2)}, u32[]{:S(2)}) async-start(bf16[4,8,128,576]{2,1,3,0:T(8,128)(2,1)} %copy.84), calls=%async_computation.3 | async-start | bytes 9437184 | tf_op jit(solution)/shard_map/all_to_all | solution.py:31
  51.5 96.7 %all-to-all-done.3 = bf16[4,8,128,576]{2,1,3,0:T(8,128)(2,1)} async-done(((bf16[4,8,128,576]{2,1,3,0:T(8,128)(2,1)}), bf16[4,8,128,576]{2,1,3,0:T(8,128)(2,1)}, u32[]{:S(2)}, u32[]{:S(2)}) %all-to-all-start.3) | async-done | bytes 4718624 | tf_op jit(solution)/shard_map/all_to_all | solution.py:31
  148.2 3.4 %copy.85 = bf16[4,8,128,576]{2,3,1,0:T(8,128)(2,1)S(1)} copy(bf16[4,8,128,576]{2,1,3,0:T(8,128)(2,1)} %all-to-all-done.3) | data formatting | bytes 9437184 | tf_op jit(solution)/shard_map/all_to_all | solution.py:31
  151.6 5.2 %pad_maximum_fusion = bf16[48,128,576]{1,2,0:T(8,128)(2,1)} fusion(bf16[32,128,576]{1,2,0:T(8,128)(2,1)S(1)} %bitcast.95, bf16[16,128,576]{1,2,0:T(8,128)(2,1)} %param.17), kind=kLoop, calls=%fused_computation.37 | loop fusion | flops 3538944 | bytes 14155776 | tf_op jit(solution)/shard_map/concatenate | solution.py:150
  156.8 114.6 %while.14 = (s32[]{:T(128)}, f32[2,64]{1,0:T(2,128)S(1)}, f32[2,64]{1,0:T(2,128)}, f32[2,64,512]{2,0,1:T(2,128)}, s32[6,8]{1,0:T(8,128)}, /*index=5*/s32[6,8]{1,...) while((s32[]{:T(128)}, f32[2,64]{1,0:T(2,128)S(1)}, f32[2,64]{1,0:T(2,128)}, ...), condition=%wide.region_10.11_spmd, body=%wide.region_6.10_spmd.sunk | while | flops 144676848 | bytes 8751429 | solution.py:119
  160.1 2.4 gather_fusion
  168.0 2.3 fusion.76
  173.7 2.2 convolution_add_fusion.5
  179.2 2.4 gather_fusion
  187.1 2.3 fusion.76
  192.8 2.2 convolution_add_fusion.5
  198.3 2.4 gather_fusion
  206.2 2.3 fusion.76
  211.9 2.2 convolution_add_fusion.5
  217.4 2.4 gather_fusion
  225.3 2.3 fusion.76
  230.9 2.2 convolution_add_fusion.5
  236.5 2.4 gather_fusion
  244.4 2.3 fusion.76
  250.0 2.2 convolution_add_fusion.5
  255.6 2.4 gather_fusion
  263.5 2.3 fusion.76
  272.6 8.5 %all_to_all.61 = bf16[2,4,16,512]{3,1,0,2:T(4,128)(2,1)S(1)} all-to-all(bf16[2,4,16,512]{3,1,0,2:T(4,128)(2,1)S(1)} %copy.88), channel_id=1, replica_groups=mesh['groups'=2,'dev'=4,'pd'=4] {'dev'}, dimensions={2} | all-to-all | bytes 262144 | tf_op jit(solution)/shard_map/all_to_all | solution.py:158
  282.5 5.2 %convolution_convert_fusion = bf16[32,7168]{1,0:T(8,128)(2,1)} fusion(bf16[512,7168]{1,0:T(8,128)(2,1)} %param.21, bf16[4,8,4,128]{3,2,1,0:T(4,128)(2,1)S(1)} %bitcast.102), kind=kOutput, calls=%fused_computation.36 | convolution fusion | flops 235110400 | bytes 7831552 | tf_op jit(solution)/shard_map/dot_general | solution.py:164
  287.7 20.2 %reduce-scatter.2.cloned.1.call-done = bf16[8,7168]{1,0:T(8,128)(2,1)} async-done(((bf16[32,7168]{1,0:T(8,128)(2,1)}), bf16[8,7168]{1,0:T(8,128)(2,1)}) %reduce-scatter.2.cloned.1.call-update) | async-done | bytes 114704 | tf_op jit(solution)/shard_map/reduce_scatter | solution.py:163
  (167 shorter events, 90.3 us)
Async XLA Ops:
  6.5 25.9 %copy-start = (bf16[16,128,576]{1,2,0:T(8,128)(2,1)S(1)}, bf16[16,128,576]{1,2,0:T(8,128)(2,1)}, u32[]{:S(2)}) copy-start(bf16[16,128,576]{1,2,0:T(8,128)(2,1)} %param.14) | copy-start | bytes 7077892
  8.2 12.1 %all-to-all-start = ((bf16[2,4,16,192]{3,1,0,2:T(4,128)(2,1)}), bf16[2,4,16,192]{3,1,0,2:T(4,128)(2,1)S(1)}, u32[]{:S(2)}, u32[]{:S(2)}) async-start(bf16[2,4,16,192]{3,1,0,2:T(4,128)(2,1)} %copy.77), calls=%async_computation | async-start | bytes 131072 | tf_op jit(solution)/shard_map/all_to_all | solution.py:139
  20.3 8.8 %all-to-all-start.2 = ((s32[4,8,3]{1,2,0:T(4,128)}), s32[4,8,3]{1,2,0:T(4,128)S(1)}, u32[]{:S(2)}, u32[]{:S(2)}) async-start(s32[4,8,3]{1,2,0:T(4,128)} %copy.81), calls=%async_computation.2 | async-start | bytes 16384 | tf_op jit(solution)/shard_map/all_to_all | solution.py:38
  29.1 11.8 %all-to-all-start.1 = ((bf16[8,4,4,576]{3,1,2,0:T(4,128)(2,1)}), bf16[8,4,4,576]{3,1,2,0:T(4,128)(2,1)S(1)}, u32[]{:S(2)}, u32[]{:S(2)}) async-start(bf16[8,4,4,576]{3,1,2,0:T(4,128)(2,1)} %copy.79), calls=%async_computation.1 | async-start | bytes 327680 | tf_op jit(solution)/shard_map/all_to_all | solution.py:144
  40.9 5.3 %copy-start.4 = (s32[16]{0:T(128)S(1)}, s32[16]{0:T(128)}, u32[]{:S(2)}) copy-start(s32[16]{0:T(128)} %param.18) | copy-start | bytes 196
  40.9 6.1 %copy-start.5 = (s32[2]{0:T(128)S(1)}, s32[2]{0:T(128)}, u32[]{:S(2)}) copy-start(s32[2]{0:T(128)} %param.16) | copy-start | bytes 28
  40.9 7.7 %copy-start.1 = (bf16[2,4,576]{2,1,0:T(4,128)(2,1)S(1)}, bf16[2,4,576]{2,1,0:T(4,128)(2,1)}, u32[]{:S(2)}) copy-start(bf16[2,4,576]{2,1,0:T(4,128)(2,1)} %param.13) | copy-start | bytes 27652
  40.9 107.3 %all-to-all-start.3 = ((bf16[4,8,128,576]{2,1,3,0:T(8,128)(2,1)}), bf16[4,8,128,576]{2,1,3,0:T(8,128)(2,1)}, u32[]{:S(2)}, u32[]{:S(2)}) async-start(bf16[4,8,128,576]{2,1,3,0:T(8,128)(2,1)} %copy.84), calls=%async_computation.3 | async-start | bytes 9437184 | tf_op jit(solution)/shard_map/all_to_all | solution.py:31
  46.1 261.9 %reduce-scatter.2.cloned.1.call-start = ((), (), s32[]{:S(2)}) async-start(), calls=%async_computation.6 | async-start | bytes 573440 | tf_op jit(solution)/shard_map/reduce_scatter | solution.py:163
  159.5 0.5 copy-start.2
  162.5 3.6 %copy-start.3 = (pred[8,2]{0,1:T(4,128)(4,1)S(1)}, pred[8,2]{0,1:T(4,128)(4,1)}, u32[]{:S(2)}) copy-start(pred[8,2]{0,1:T(4,128)(4,1)} %iota_compare_fusion.12) | copy-start | bytes 52 | tf_op jit(solution)/shard_map/while
  178.6 0.5 copy-start.2
  181.6 3.6 %copy-start.3 = (pred[8,2]{0,1:T(4,128)(4,1)S(1)}, pred[8,2]{0,1:T(4,128)(4,1)}, u32[]{:S(2)}) copy-start(pred[8,2]{0,1:T(4,128)(4,1)} %iota_compare_fusion.12) | copy-start | bytes 52 | tf_op jit(solution)/shard_map/while
  197.7 0.5 copy-start.2
  200.7 3.6 %copy-start.3 = (pred[8,2]{0,1:T(4,128)(4,1)S(1)}, pred[8,2]{0,1:T(4,128)(4,1)}, u32[]{:S(2)}) copy-start(pred[8,2]{0,1:T(4,128)(4,1)} %iota_compare_fusion.12) | copy-start | bytes 52 | tf_op jit(solution)/shard_map/while
  216.8 0.5 copy-start.2
  219.8 3.6 %copy-start.3 = (pred[8,2]{0,1:T(4,128)(4,1)S(1)}, pred[8,2]{0,1:T(4,128)(4,1)}, u32[]{:S(2)}) copy-start(pred[8,2]{0,1:T(4,128)(4,1)} %iota_compare_fusion.12) | copy-start | bytes 52 | tf_op jit(solution)/shard_map/while
  235.9 0.5 copy-start.2
  238.9 3.6 %copy-start.3 = (pred[8,2]{0,1:T(4,128)(4,1)S(1)}, pred[8,2]{0,1:T(4,128)(4,1)}, u32[]{:S(2)}) copy-start(pred[8,2]{0,1:T(4,128)(4,1)} %iota_compare_fusion.12) | copy-start | bytes 52 | tf_op jit(solution)/shard_map/while
  255.0 0.5 copy-start.2
  258.0 3.6 %copy-start.3 = (pred[8,2]{0,1:T(4,128)(4,1)S(1)}, pred[8,2]{0,1:T(4,128)(4,1)}, u32[]{:S(2)}) copy-start(pred[8,2]{0,1:T(4,128)(4,1)} %iota_compare_fusion.12) | copy-start | bytes 52 | tf_op jit(solution)/shard_map/while
Sparse Core Ops, SparseCore 0:
  287.8 20.0 reduce-scatter.1
where the time goes:
time: 317 us; the launch traced here: 315 us
  waiting for transfers between devices  123 us (39%)
  matrix products  63.2 us (20%)
  local copies, waits for them, and re-layouts  48.8 us (15%)
  other arithmetic  39.7 us (13%)
  starting transfers between devices  18.1 us (6%)
  between operations  13.6 us (4%)
  blocking collectives  8.46 us (3%)
    all_to_all x1, waiting for transfers between devices, deliver(): lax.all_to_all(outgoing.reshape(devices, per_pair, width, -1), 'dev', spl...  96.7 us
    reduce_scatter x1, waiting for transfers between devices, shards(): lax.psum_scatter(jnp.dot(flat, output_weight, preferred_element_type=jnp....  20.2 us
    gather x6, local copies, waits for them, and re-layouts, advance(): picked = jnp.take(queries, block_owner, axis=0)  14.2 us
    dot_general x6, matrix products, advance(): jnp.einsum('gqk,gkc->gqc', weight.astype(jnp.bfloat16), block_keys[..., :...  13.6 us
    dot_general x6, matrix products, advance(): accum = accum * factor[..., None] + jnp.einsum('gr,gqc->rqc', ownf, carried)  13.4 us
    dot_general x6, matrix products, advance(): jnp.einsum('gqc,gkc->gqk', picked, block_keys, preferred_element_type=jnp...  13.2 us
    all_to_all x1, blocking collectives, shards(): lax.all_to_all(latent_out, 'dev', split_axis=2, concat_axis=0, tiled=True)  8.46 us
    dot_general x6, matrix products, advance(): mass = jnp.einsum('gr,gq->rq', ownf, jnp.sum(weight, axis=2))  8.3 us
  transfers between devices with their start and end apart: 5, of which 4 were waited for; matrix products, arithmetic and copies ran while one was open for 6% of the time, Pallas kernels for 0%

commit v1 on v0

--- a/solution.py
+++ b/solution.py
@@ -1,8 +1,11 @@
+import functools
 import math
 
 import jax
 import jax.numpy as jnp
 from jax import lax
+from jax.experimental import pallas as pl
+from jax.experimental.pallas import tpu as pltpu
 from jax.sharding import PartitionSpec as P
 
 KVR = 512
@@ -120,7 +123,7 @@
     return state
 
 
-def shards(
+def routed_shards(
     queries,
     new_latents,
     prompt_blocks,
@@ -169,7 +172,367 @@
     return mixed
 
 
+DEVS = 4
+CHUNK = 1024
+FAR = -1e30
+MESH = pl.DeviceIdType.MESH
+
+
+def partner(me, step):
+    return (me, me + 1 - 2 * (me % 2), (me + 2) % 4, 3 - me)[step]
+
+
+def still_kernel(
+    routes,
+    slots,
+    lengths,
+    queries,
+    fresh,
+    prompt_hbm,
+    resident_hbm,
+    absorb_hbm,
+    expand_hbm,
+    output_hbm,
+    out,
+    keys,
+    absorb,
+    expand,
+    weight,
+    asked,
+    lens,
+    absorbed,
+    bias,
+    scores,
+    partial,
+    stats,
+    landed,
+    landed_stats,
+    mixed,
+    landed_mixed,
+    local_sem,
+    q_send,
+    q_recv,
+    n_send,
+    n_recv,
+    a_send,
+    a_recv,
+    o_send,
+    o_recv,
+    t_send,
+    t_recv,
+    y_send,
+    y_recv,
+    *,
+    scale,
+):
+    me = lax.axis_index("dev")
+    prompt_rows = prompt_hbm.shape[0]
+    home_rows = resident_hbm.shape[0]
+    block = 128
+    new_rows = fresh.shape[0]
+    heads, nope, rank = absorb.shape
+    lat = keys.shape[1]
+    own = queries.shape[1] // heads
+    rows = DEVS * own
+    span = heads * rows
+    steps = new_rows // lengths.shape[0]
+    requests = lengths.shape[0]
+
+    loads = [
+        pltpu.make_async_copy(absorb_hbm, absorb, local_sem.at[0]),
+        pltpu.make_async_copy(prompt_hbm, keys.at[pl.ds(0, prompt_rows)], local_sem.at[1]),
+        pltpu.make_async_copy(resident_hbm, keys.at[pl.ds(prompt_rows, home_rows)], local_sem.at[2]),
+        pltpu.make_async_copy(expand_hbm, expand, local_sem.at[3]),
+        pltpu.make_async_copy(output_hbm, weight, local_sem.at[4]),
+    ]
+    for load in loads:
+        load.start()
+
+    barrier = pltpu.get_barrier_semaphore()
+    for step in range(1, DEVS):
+        pl.semaphore_signal(barrier, inc=1, device_id={"dev": partner(me, step)}, device_id_type=MESH)
+    pl.semaphore_wait(barrier, DEVS - 1)
+
+    def remote(source, target, send, recv, step):
+        return pltpu.make_async_remote_copy(
+            src_ref=source,
+            dst_ref=target,
+            send_sem=send,
+            recv_sem=recv,
+            device_id={"dev": partner(me, step)},
+            device_id_type=MESH,
+        )
+
+    sent = []
+
+    def launch(copy):
+        copy.start()
+        sent.append(copy)
+        return copy
+
+    asks = {}
+    for step in (3, 2, 1):
+        asks[step] = launch(
+            remote(queries.at[partner(me, step)], asked.at[step], q_send.at[step], q_recv.at[step], step)
+        )
+    request_row = lax.broadcasted_iota(jnp.int32, (own, 128), 0) // steps
+    length_rows = jnp.zeros((own, 128), jnp.int32)
+    for r in range(requests):
+        length_rows = jnp.where(request_row == r, lengths[r], length_rows)
+    lens[0] = length_rows
+    counts = {}
+    for step in (3, 2, 1):
+        counts[step] = launch(remote(lens.at[0], lens.at[step], n_send.at[step], n_recv.at[step], step))
+
+    asked[0] = queries[me]
+    padding = jnp.zeros((block - new_rows, lat), jnp.float32)
+    keys[pl.ds(prompt_rows + home_rows, block), :] = jnp.concatenate(
+        [fresh[...].astype(jnp.float32), padding], axis=0
+    ).astype(keys.dtype)
+
+    for step in (1, 2, 3):
+        asks[step].wait_recv()
+    loads[0].wait()
+    asking = [asked[step].astype(jnp.float32) for step in range(DEVS)]
+    for head in range(heads):
+        piece = jnp.concatenate([a[head * own : (head + 1) * own] for a in asking], axis=0).astype(
+            jnp.bfloat16
+        )
+        latent = jnp.dot(piece[:, :nope], absorb[head], preferred_element_type=jnp.float32)
+        absorbed[0, pl.ds(head * rows, rows), 0:rank] = latent.astype(jnp.bfloat16)
+        absorbed[0, pl.ds(head * rows, rows), rank:lat] = piece[:, nope:]
+    shares = {}
+    for step in (1, 3, 2):
+        shares[step] = launch(
+            remote(absorbed.at[0], absorbed.at[step], a_send.at[step], a_recv.at[step], step)
+        )
+
+    for step in (1, 2, 3):
+        counts[step].wait_recv()
+    lane = lax.broadcasted_iota(jnp.int32, (rows, block), 1)
+    row = lax.broadcasted_iota(jnp.int32, (rows, block), 0)
+    row_length = jnp.concatenate([lens[step] for step in range(DEVS)], axis=0)
+    row_device = jnp.zeros((rows, block), jnp.int32)
+    for step in range(DEVS):
+        row_device = jnp.where(row // own == step, partner(me, step), row_device)
+    row_request = row_device * requests + (row % own) // steps
+    for b in range(prompt_rows // block):
+        owner = routes[3 * b] * requests + routes[3 * b + 1]
+        seen = (row_request == owner) & (routes[3 * b + 2] * block + lane < row_length)
+        bias[:, pl.ds(b * block, block)] = jnp.where(seen, 0.0, FAR)
+    for b in range(home_rows // block):
+        seen = row_request == me * requests + slots[b]
+        bias[:, pl.ds(prompt_rows + b * block, block)] = jnp.where(seen, 0.0, FAR)
+    seen = (
+        (row_request == me * requests + lane // steps)
+        & (lane % steps <= row % steps)
+        & (lane < new_rows)
+    )
+    total_rows = prompt_rows + home_rows + block
+    bias[:, pl.ds(prompt_rows + home_rows, block)] = jnp.where(seen, 0.0, FAR)
+    loads[1].wait()
+    loads[2].wait()
+
+    cuts = [(at, min(CHUNK, total_rows - at)) for at in range(0, total_rows, CHUNK)]
+    for step in (0, 1, 3, 2):
+        if step:
+            shares[step].wait_recv()
+        shard = absorbed[step]
+        top = jnp.full((span, 1), FAR, jnp.float32)
+        order = [s ^ step for s in range(DEVS)]
+        for at, size in cuts:
+            piece = lax.dot_general(
+                shard,
+                keys[pl.ds(at, size), :],
+                (((1,), (1,)), ((), ())),
+                preferred_element_type=jnp.float32,
+            )
+            mask = jnp.concatenate(
+                [bias[s * own : (s + 1) * own, at : at + size] for s in order], axis=0
+            )
+            piece = (piece * scale).reshape(heads, rows, size) + mask[None]
+            piece = piece.reshape(span, size)
+            scores[:, pl.ds(at, size)] = piece
+            top = jnp.maximum(top, jnp.max(piece, axis=1, keepdims=True))
+        total = jnp.zeros((span, 1), jnp.float32)
+        summed = jnp.zeros((span, rank), jnp.float32)
+        for at, size in cuts:
+            live = jnp.exp(scores[:, pl.ds(at, size)] - top)
+            total = total + jnp.sum(live, axis=1, keepdims=True)
+            summed = summed + jnp.dot(
+                live.astype(jnp.bfloat16),
+                keys[pl.ds(at, size), 0:rank],
+                preferred_element_type=jnp.float32,
+            )
+        result = (summed / total).astype(jnp.bfloat16)
+        top_row = jnp.transpose(jnp.broadcast_to(top, (span, 128)))[0:8]
+        total_row = jnp.transpose(jnp.broadcast_to(total, (span, 128)))[0:8]
+        if step:
+            partial[step] = result
+            stats[step, 0:8, :] = top_row
+            stats[step, 8:16, :] = total_row
+            launch(remote(stats.at[step], landed_stats.at[step], t_send.at[step], t_recv.at[step], step))
+            launch(remote(partial.at[step], landed.at[step], o_send.at[step], o_recv.at[step], step))
+        else:
+            landed[0] = result
+            landed_stats[0, 0:8, :] = top_row
+            landed_stats[0, 8:16, :] = total_row
+
+    for step in (1, 3, 2):
+        remote(stats.at[step], landed_stats.at[step], t_send.at[step], t_recv.at[step], step).wait_recv()
+        remote(partial.at[step], landed.at[step], o_send.at[step], o_recv.at[step], step).wait_recv()
+    tops = [
+        jnp.transpose(jnp.broadcast_to(landed_stats[s, 0:1, :], (128, span)))[:, 0:1] for s in range(DEVS)
+    ]
+    totals = [
+        jnp.transpose(jnp.broadcast_to(landed_stats[s, 8:9, :], (128, span)))[:, 0:1] for s in range(DEVS)
+    ]
+    best = functools.reduce(jnp.maximum, tops)
+    parts = [t * jnp.exp(m - best) for m, t in zip(tops, totals)]
+    whole = functools.reduce(jnp.add, parts)
+    latent_out = functools.reduce(
+        jnp.add, [landed[s].astype(jnp.float32) * (parts[s] / whole) for s in range(DEVS)]
+    ).astype(jnp.bfloat16)
+    loads[3].wait()
+    expanded = jnp.concatenate(
+        [
+            jnp.dot(
+                latent_out[head * rows : (head + 1) * rows],
+                expand[head],
+                preferred_element_type=jnp.float32,
+            ).astype(jnp.bfloat16)
+            for head in range(heads)
+        ],
+        axis=1,
+    )
+    loads[4].wait()
+    half = out.shape[1] // 2
+    pieces = y_send.shape[1]
+    wide = half // pieces
+    for c in range(pieces):
+        low = jnp.dot(expanded, weight[:, pl.ds(c * wide, wide)], preferred_element_type=jnp.float32)
+        high = jnp.dot(
+            expanded, weight[:, pl.ds(half + c * wide, wide)], preferred_element_type=jnp.float32
+        )
+        for step in (3, 2, 1, 0):
+            both = jnp.concatenate(
+                [low[step * own : (step + 1) * own], high[step * own : (step + 1) * own]], axis=0
+            )
+            mixed[step, :, pl.ds(c * wide, wide)] = both.astype(jnp.bfloat16)
+            if step:
+                launch(
+                    remote(
+                        mixed.at[step, :, pl.ds(c * wide, wide)],
+                        landed_mixed.at[step, :, pl.ds(c * wide, wide)],
+                        y_send.at[step, c],
+                        y_recv.at[step, c],
+                        step,
+                    )
+                )
+    for c in range(pieces):
+        both = mixed[0, :, pl.ds(c * wide, wide)].astype(jnp.float32)
+        for step in (1, 2, 3):
+            remote(
+                mixed.at[step, :, pl.ds(c * wide, wide)],
+                landed_mixed.at[step, :, pl.ds(c * wide, wide)],
+                y_send.at[step, c],
+                y_recv.at[step, c],
+                step,
+            ).wait_recv()
+            both = both + landed_mixed[step, :, pl.ds(c * wide, wide)].astype(jnp.float32)
+        out[:, pl.ds(c * wide, wide)] = both[0:own].astype(jnp.bfloat16)
+        out[:, pl.ds(half + c * wide, wide)] = both[own : 2 * own].astype(jnp.bfloat16)
+    for copy in sent:
+        copy.wait_send()
+
+
+def still_shards(
+    queries,
+    new_latents,
+    prompt_blocks,
+    block_routes,
+    prompt_lengths,
+    resident_blocks,
+    resident_slots,
+    key_absorb,
+    value_expand,
+    output_weight,
+):
+    requests, steps, all_heads, width = queries.shape
+    heads = key_absorb.shape[0]
+    lat = prompt_blocks.shape[2]
+    prompt_rows = prompt_blocks.shape[0] * prompt_blocks.shape[1]
+    home_rows = resident_blocks.shape[0] * resident_blocks.shape[1]
+    total_rows = prompt_rows + home_rows + 128
+    own = requests * steps
+    rows = DEVS * own
+    span = heads * rows
+    rank = key_absorb.shape[2]
+    model = output_weight.shape[1]
+    pieces = 4
+    by_head = (
+        queries.reshape(own, DEVS, heads, width).transpose(1, 2, 0, 3).reshape(DEVS, heads * own, width)
+    )
+    smem = pl.BlockSpec(memory_space=pltpu.SMEM)
+    vmem = pl.BlockSpec(memory_space=pltpu.VMEM)
+    held = pl.BlockSpec(memory_space=pl.ANY)
+    pair = pltpu.SemaphoreType.DMA((DEVS,))
+    bf16 = jnp.bfloat16
+    return pl.pallas_call(
+        functools.partial(still_kernel, scale=1.0 / math.sqrt(width)),
+        out_shape=jax.ShapeDtypeStruct((own, model), bf16),
+        in_specs=[smem, smem, smem, vmem, vmem, held, held, held, held, held],
+        out_specs=vmem,
+        scratch_shapes=[
+            pltpu.VMEM((total_rows, lat), bf16),
+            pltpu.VMEM(key_absorb.shape, bf16),
+            pltpu.VMEM(value_expand.shape, bf16),
+            pltpu.VMEM(output_weight.shape, bf16),
+            pltpu.VMEM((DEVS, heads * own, width), bf16),
+            pltpu.VMEM((DEVS, own, 128), jnp.int32),
+            pltpu.VMEM((DEVS, span, lat), bf16),
+            pltpu.VMEM((rows, total_rows), jnp.float32),
+            pltpu.VMEM((span, total_rows), jnp.float32),
+            pltpu.VMEM((DEVS, span, rank), bf16),
+            pltpu.VMEM((DEVS, 16, span), jnp.float32),
+            pltpu.VMEM((DEVS, span, rank), bf16),
+            pltpu.VMEM((DEVS, 16, span), jnp.float32),
+            pltpu.VMEM((DEVS, 2 * own, model // 2), bf16),
+            pltpu.VMEM((DEVS, 2 * own, model // 2), bf16),
+            pltpu.SemaphoreType.DMA((5,)),
+            pair,
+            pair,
+            pair,
+            pair,
+            pair,
+            pair,
+            pair,
+            pair,
+            pair,
+            pair,
+            pltpu.SemaphoreType.DMA((DEVS, pieces)),
+            pltpu.SemaphoreType.DMA((DEVS, pieces)),
+        ],
+        compiler_params=pltpu.CompilerParams(
+            collective_id=0, has_side_effects=True, vmem_limit_bytes=48 * 1024 * 1024
+        ),
+        name="still_attention",
+    )(
+        block_routes.reshape(-1),
+        resident_slots,
+        prompt_lengths,
+        by_head,
+        new_latents.reshape(own, lat),
+        prompt_blocks.reshape(prompt_rows, lat),
+        resident_blocks.reshape(home_rows, lat),
+        key_absorb,
+        value_expand,
+        output_weight,
+    )
+
+
 def solution(mesh):
+    body = still_shards if mesh.shape["dev"] == DEVS else routed_shards
     in_specs = (
         P(("groups", "dev", "pd"), None, None, None),
         P(("groups", "dev", "pd"), None, None),
@@ -183,4 +546,4 @@
         P("dev", None),
     )
     out_specs = P(("groups", "dev", "pd"), None)
-    return jax.shard_map(shards, mesh=mesh, in_specs=in_specs, out_specs=out_specs, check_vma=False)
+    return jax.shard_map(body, mesh=mesh, in_specs=in_specs, out_specs=out_specs, check_vma=False)

time: 317 us -> 59.7 us (0.19)
  waiting for transfers between devices: 123 us -> 0 us
  matrix products: 63.2 us -> 0 us
  Pallas kernels: 0 us -> 47.7 us
  other arithmetic: 39.7 us -> 0 us
  local copies, waits for them, and re-layouts: 48.8 us -> 11.6 us
  starting transfers between devices: 18.1 us -> 0 us
  between operations: 13.6 us -> 0.06 us
  blocking collectives: 8.46 us -> 0 us
    all_to_all x4 -> x0, waiting for transfers between devices: 103 us -> none  [the longest x1 96.7 us: deliver(): lax.all_to_all(outgoing.reshape(devices, per_pair, width, -1), 'dev', spl...]
    dot_general x30 -> x0, matrix products: 63.2 us -> none  [the longest x6 13.6 us: advance(): jnp.einsum('gqk,gkc->gqc', weight.astype(jnp.bfloat16), block_keys[..., :...]
    pallas_call x0 -> x1, Pallas kernels: none -> 47.7 us  [still_shards(): pl.pallas_call(functools.partial(still_kernel, scale=1.0 / math.sqrt(widt...]
    reduce_scatter x1 -> x0, waiting for transfers between devices: 20.2 us -> none  [shards(): lax.psum_scatter(jnp.dot(flat, output_weight, preferred_element_type=jnp....]
    all_to_all x4 -> x0, starting transfers between devices: 18.1 us -> none  [the longest x1 6.32 us: shards(): lax.all_to_all(queries, 'dev', split_axis=2, concat_axis=0, tiled=True)]
    gather x12 -> x0, local copies, waits for them, and re-layouts: 17.5 us -> none  [the longest x6 14.2 us: advance(): picked = jnp.take(queries, block_owner, axis=0)]
    squeeze x8 -> x0, local copies, waits for them, and re-layouts: 8.79 us -> none  [the longest x6 8.1 us: sweep(): state, unused = lax.scan(advance, state, grouped)]
    select_n x13 -> x0, other arithmetic: 8.67 us -> none  [the longest x6 4.51 us: advance(): jnp.take(new_top, block_owner, axis=0)[:, :, None]]
  transfers between devices with their start and end apart: 5 -> 0, of which waited for: 4 -> 0; matrix products, arithmetic and copies ran while one was open for 6% -> 0% of each run, Pallas kernels for 0% -> 0%
where the time goes in v1:
time: 59.7 us; the launch traced here: 59.3 us
  Pallas kernels  47.7 us (80%)
  local copies, waits for them, and re-layouts  11.6 us (19%)
    pallas_call x1, Pallas kernels, still_shards(): pl.pallas_call(functools.partial(still_kernel, scale=1.0 / math.sqrt(widt...  47.7 us
    unnamed x12, local copies, waits for them, and re-layouts  9.93 us

profile of v1, /device:TPU:0, one launch (start us, length us, event | category | flops | bytes accessed | tf_op | source)
XLA Modules:
  0.0 59.3 jit_solution(15086421759707753479)
XLA Ops:
  0.0 0.8 %copy.15 = s32[16,3]{1,0:T(8,128)S(1)} copy(s32[16,3]{0,1:T(4,128)} %param.13) | data formatting | bytes 384 | tf_op args[3]
  0.8 0.1 reshape.18.routes
  0.8 0.7 %reshape.21.fresh = bf16[8,576]{1,0:T(8,128)(2,1)S(1)} reshape(bf16[2,4,576]{2,1,0:T(4,128)(2,1)} %param.11) | data formatting | bytes 18432 | tf_op jit(solution)/shard_map/reshape | solution.py:525
  1.6 0.9 %reshape.19 = bf16[8,4,4,192]{3,2,1,0:T(4,128)(2,1)S(1)} reshape(bf16[2,4,16,192]{3,2,1,0:T(8,128)(2,1)} %param.10) | data formatting | bytes 98304 | tf_op jit(solution)/shard_map/reshape | solution.py:474
  2.5 3.1 %copy.17 = bf16[16,128,576]{2,1,0:T(8,128)(2,1)S(1)} copy(bf16[16,128,576]{1,2,0:T(8,128)(2,1)} %param.12) | data formatting | bytes 4718592 | tf_op args[2]
  5.6 0.0 copy-start
  5.6 0.0 copy-start.2
  5.6 0.0 copy-start.3
  5.6 4.4 %copy.18 = bf16[16,128,576]{2,1,0:T(8,128)(2,1)} copy(bf16[16,128,576]{1,2,0:T(8,128)(2,1)} %param.15) | data formatting | bytes 4718592 | tf_op args[5]
  10.0 0.0 copy-done
  10.0 0.0 copy-done.2
  10.0 0.0 copy-done.3
  10.0 0.0 copy-start.1
  10.0 1.0 %copy-done.1 = bf16[4,512,128]{2,1,0:T(8,128)(2,1)S(1)} copy-done((bf16[4,512,128]{2,1,0:T(8,128)(2,1)S(1)}, bf16[4,512,128]{2,1,0:T(8,128)(2,1)}, u32[]{:S(2)}) %copy-start.1) | copy-done | bytes 524312
  11.0 47.7 %still_attention.1 = bf16[8,7168]{1,0:T(8,128)(2,1)S(1)} custom-call(s32[48]{0:T(128)S(1)} %reshape.18.routes, s32[16]{0:T(128)S(1)} %copy-done.2, s32[2]{0:T(128)S(1)} %copy-done.3, bf16[4,32,192]{2,1,0:T(8,128)(2,1)S(1)} %bitcast.10, bf16[8,576]{1,0:T(8,128)(2,1)S(1)} %reshape.21.fresh, bf16[2048,576]{1,0:T(8,128)(2,1)S(1)} %bitcast.9, ...), custom_call_target="tpu_custom_call" | custom-call | tf_op jit(solution)/shard_map/still_attention/pallas_call | solution.py:481
  58.7 0.6 %copy.22 = bf16[8,7168]{1,0:T(8,128)(2,1)} copy(bf16[8,7168]{1,0:T(8,128)(2,1)S(1)} %still_attention.1) | data formatting | bytes 229376
  (1 shorter events, 0.0 us)
Async XLA Ops:
  5.6 4.4 %copy-start = (bf16[4,128,512]{2,1,0:T(8,128)(2,1)S(1)}, bf16[4,128,512]{2,1,0:T(8,128)(2,1)}, u32[]{:S(2)}) copy-start(bf16[4,128,512]{2,1,0:T(8,128)(2,1)} %absorb_hbm.1) | copy-start | bytes 1572868
  5.6 4.4 %copy-start.2 = (s32[16]{0:T(128)S(1)}, s32[16]{0:T(128)}, u32[]{:S(2)}) copy-start(s32[16]{0:T(128)} %slots.1) | copy-start | bytes 196
  5.6 4.4 %copy-start.3 = (s32[2]{0:T(128)S(1)}, s32[2]{0:T(128)}, u32[]{:S(2)}) copy-start(s32[2]{0:T(128)} %lengths.1) | copy-start | bytes 28
  10.0 1.0 %copy-start.1 = (bf16[4,512,128]{2,1,0:T(8,128)(2,1)S(1)}, bf16[4,512,128]{2,1,0:T(8,128)(2,1)}, u32[]{:S(2)}) copy-start(bf16[4,512,128]{2,1,0:T(8,128)(2,1)} %expand_hbm.1) | copy-start | bytes 1572868

commit v2 on v1

--- a/solution.py
+++ b/solution.py
@@ -186,14 +186,19 @@
     routes,
     slots,
     lengths,
-    queries,
-    fresh,
+    queries_hbm,
+    fresh_hbm,
     prompt_hbm,
     resident_hbm,
     absorb_hbm,
     expand_hbm,
     output_hbm,
     out,
+    queries,
+    spread,
+    spread_rope,
+    by_head,
+    fresh,
     keys,
     absorb,
     expand,
@@ -210,6 +215,7 @@
     mixed,
     landed_mixed,
     local_sem,
+    block_sem,
     q_send,
     q_recv,
     n_send,
@@ -226,26 +232,30 @@
     scale,
 ):
     me = lax.axis_index("dev")
-    prompt_rows = prompt_hbm.shape[0]
-    home_rows = resident_hbm.shape[0]
-    block = 128
-    new_rows = fresh.shape[0]
+    held, lat, block = prompt_hbm.shape
+    homes = resident_hbm.shape[0]
+    prompt_rows = held * block
+    home_rows = homes * block
     heads, nope, rank = absorb.shape
-    lat = keys.shape[1]
-    own = queries.shape[1] // heads
+    requests, steps, all_heads, width = queries.shape
+    own = requests * steps
+    new_rows = own
     rows = DEVS * own
     span = heads * rows
-    steps = new_rows // lengths.shape[0]
-    requests = lengths.shape[0]
 
     loads = [
-        pltpu.make_async_copy(absorb_hbm, absorb, local_sem.at[0]),
-        pltpu.make_async_copy(prompt_hbm, keys.at[pl.ds(0, prompt_rows)], local_sem.at[1]),
-        pltpu.make_async_copy(resident_hbm, keys.at[pl.ds(prompt_rows, home_rows)], local_sem.at[2]),
+        pltpu.make_async_copy(queries_hbm, queries, local_sem.at[0]),
+        pltpu.make_async_copy(absorb_hbm, absorb, local_sem.at[1]),
+        pltpu.make_async_copy(fresh_hbm, fresh, local_sem.at[2]),
         pltpu.make_async_copy(expand_hbm, expand, local_sem.at[3]),
         pltpu.make_async_copy(output_hbm, weight, local_sem.at[4]),
     ]
-    for load in loads:
+    blocks = [
+        pltpu.make_async_copy(source.at[b], keys.at[:, pl.ds((first + b) * block, block)], block_sem.at[first + b])
+        for source, count, first in ((prompt_hbm, held, 0), (resident_hbm, homes, held))
+        for b in range(count)
+    ]
+    for load in loads[:3] + blocks + loads[3:]:
         load.start()
 
     barrier = pltpu.get_barrier_semaphore()
@@ -270,10 +280,22 @@
         sent.append(copy)
         return copy
 
+    loads[0].wait()
+    for r in range(own):
+        rows_now = queries[r // steps, r % steps].astype(jnp.float32)
+        for ref, at in ((spread, 0), (spread_rope, nope)):
+            part = rows_now[:, at : at + nope]
+            if part.shape[1] < nope:
+                part = jnp.concatenate([part, jnp.zeros((all_heads, nope - part.shape[1]), jnp.float32)], axis=1)
+            ref[pl.ds(r, all_heads, stride=own), :] = part
+    by_head[:, :, 0:nope] = spread[...].astype(jnp.bfloat16).reshape(DEVS, heads * own, nope)
+    by_head[:, :, nope:width] = (
+        spread_rope[:, 0 : width - nope].astype(jnp.bfloat16).reshape(DEVS, heads * own, width - nope)
+    )
     asks = {}
     for step in (3, 2, 1):
         asks[step] = launch(
-            remote(queries.at[partner(me, step)], asked.at[step], q_send.at[step], q_recv.at[step], step)
+            remote(by_head.at[partner(me, step)], asked.at[step], q_send.at[step], q_recv.at[step], step)
         )
     request_row = lax.broadcasted_iota(jnp.int32, (own, 128), 0) // steps
     length_rows = jnp.zeros((own, 128), jnp.int32)
@@ -284,15 +306,16 @@
     for step in (3, 2, 1):
         counts[step] = launch(remote(lens.at[0], lens.at[step], n_send.at[step], n_recv.at[step], step))
 
-    asked[0] = queries[me]
+    asked[0] = by_head[me]
+    loads[2].wait()
+    newest = [fresh[r].astype(jnp.float32) for r in range(requests)]
     padding = jnp.zeros((block - new_rows, lat), jnp.float32)
-    keys[pl.ds(prompt_rows + home_rows, block), :] = jnp.concatenate(
-        [fresh[...].astype(jnp.float32), padding], axis=0
-    ).astype(keys.dtype)
+    newest = jnp.concatenate(newest + [padding], axis=0)
+    keys[:, pl.ds(prompt_rows + home_rows, block)] = jnp.transpose(newest).astype(keys.dtype)
 
     for step in (1, 2, 3):
         asks[step].wait_recv()
-    loads[0].wait()
+    loads[1].wait()
     asking = [asked[step].astype(jnp.float32) for step in range(DEVS)]
     for head in range(heads):
         piece = jnp.concatenate([a[head * own : (head + 1) * own] for a in asking], axis=0).astype(
@@ -317,8 +340,8 @@
         row_device = jnp.where(row // own == step, partner(me, step), row_device)
     row_request = row_device * requests + (row % own) // steps
     for b in range(prompt_rows // block):
-        owner = routes[3 * b] * requests + routes[3 * b + 1]
-        seen = (row_request == owner) & (routes[3 * b + 2] * block + lane < row_length)
+        owner = routes[0, b] * requests + routes[1, b]
+        seen = (row_request == owner) & (routes[2, b] * block + lane < row_length)
         bias[:, pl.ds(b * block, block)] = jnp.where(seen, 0.0, FAR)
     for b in range(home_rows // block):
         seen = row_request == me * requests + slots[b]
@@ -330,8 +353,8 @@
     )
     total_rows = prompt_rows + home_rows + block
     bias[:, pl.ds(prompt_rows + home_rows, block)] = jnp.where(seen, 0.0, FAR)
-    loads[1].wait()
-    loads[2].wait()
+    for load in blocks:
+        load.wait()
 
     cuts = [(at, min(CHUNK, total_rows - at)) for at in range(0, total_rows, CHUNK)]
     for step in (0, 1, 3, 2):
@@ -341,12 +364,7 @@
         top = jnp.full((span, 1), FAR, jnp.float32)
         order = [s ^ step for s in range(DEVS)]
         for at, size in cuts:
-            piece = lax.dot_general(
-                shard,
-                keys[pl.ds(at, size), :],
-                (((1,), (1,)), ((), ())),
-                preferred_element_type=jnp.float32,
-            )
+            piece = jnp.dot(shard, keys[:, pl.ds(at, size)], preferred_element_type=jnp.float32)
             mask = jnp.concatenate(
                 [bias[s * own : (s + 1) * own, at : at + size] for s in order], axis=0
             )
@@ -359,9 +377,10 @@
         for at, size in cuts:
             live = jnp.exp(scores[:, pl.ds(at, size)] - top)
             total = total + jnp.sum(live, axis=1, keepdims=True)
-            summed = summed + jnp.dot(
+            summed = summed + lax.dot_general(
                 live.astype(jnp.bfloat16),
-                keys[pl.ds(at, size), 0:rank],
+                keys[0:rank, pl.ds(at, size)],
+                (((1,), (1,)), ((), ())),
                 preferred_element_type=jnp.float32,
             )
         result = (summed / total).astype(jnp.bfloat16)
@@ -460,31 +479,32 @@
 ):
     requests, steps, all_heads, width = queries.shape
     heads = key_absorb.shape[0]
-    lat = prompt_blocks.shape[2]
-    prompt_rows = prompt_blocks.shape[0] * prompt_blocks.shape[1]
-    home_rows = resident_blocks.shape[0] * resident_blocks.shape[1]
-    total_rows = prompt_rows + home_rows + 128
+    held, block, lat = prompt_blocks.shape
+    blocks = held + resident_blocks.shape[0]
+    total_rows = (blocks + 1) * block
     own = requests * steps
     rows = DEVS * own
     span = heads * rows
     rank = key_absorb.shape[2]
     model = output_weight.shape[1]
     pieces = 4
-    by_head = (
-        queries.reshape(own, DEVS, heads, width).transpose(1, 2, 0, 3).reshape(DEVS, heads * own, width)
-    )
     smem = pl.BlockSpec(memory_space=pltpu.SMEM)
     vmem = pl.BlockSpec(memory_space=pltpu.VMEM)
-    held = pl.BlockSpec(memory_space=pl.ANY)
+    far = pl.BlockSpec(memory_space=pl.ANY)
     pair = pltpu.SemaphoreType.DMA((DEVS,))
     bf16 = jnp.bfloat16
     return pl.pallas_call(
         functools.partial(still_kernel, scale=1.0 / math.sqrt(width)),
         out_shape=jax.ShapeDtypeStruct((own, model), bf16),
-        in_specs=[smem, smem, smem, vmem, vmem, held, held, held, held, held],
+        in_specs=[smem] * 3 + [far] * 7,
         out_specs=vmem,
         scratch_shapes=[
-            pltpu.VMEM((total_rows, lat), bf16),
+            pltpu.VMEM(queries.shape, bf16),
+            pltpu.VMEM((own * all_heads, 128), jnp.float32),
+            pltpu.VMEM((own * all_heads, 128), jnp.float32),
+            pltpu.VMEM((DEVS, heads * own, width), bf16),
+            pltpu.VMEM(new_latents.shape, bf16),
+            pltpu.VMEM((lat, total_rows), bf16),
             pltpu.VMEM(key_absorb.shape, bf16),
             pltpu.VMEM(value_expand.shape, bf16),
             pltpu.VMEM(output_weight.shape, bf16),
@@ -500,6 +520,7 @@
             pltpu.VMEM((DEVS, 2 * own, model // 2), bf16),
             pltpu.VMEM((DEVS, 2 * own, model // 2), bf16),
             pltpu.SemaphoreType.DMA((5,)),
+            pltpu.SemaphoreType.DMA((blocks,)),
             pair,
             pair,
             pair,
@@ -514,17 +535,17 @@
             pltpu.SemaphoreType.DMA((DEVS, pieces)),
         ],
         compiler_params=pltpu.CompilerParams(
-            collective_id=0, has_side_effects=True, vmem_limit_bytes=48 * 1024 * 1024
+            collective_id=0, has_side_effects=True, vmem_limit_bytes=63 * 1024 * 1024
         ),
         name="still_attention",
     )(
-        block_routes.reshape(-1),
+        block_routes.T,
         resident_slots,
         prompt_lengths,
-        by_head,
-        new_latents.reshape(own, lat),
-        prompt_blocks.reshape(prompt_rows, lat),
-        resident_blocks.reshape(home_rows, lat),
+        queries,
+        new_latents,
+        prompt_blocks.transpose(0, 2, 1),
+        resident_blocks.transpose(0, 2, 1),
         key_absorb,
         value_expand,
         output_weight,

time: 59.7 us -> 51.2 us (0.86)
  local copies, waits for them, and re-layouts: 11.6 us -> 1.55 us
  Pallas kernels: 47.7 us -> 49.4 us
    unnamed x12 -> x1, local copies, waits for them, and re-layouts: 9.93 us -> 1.55 us
    pallas_call x1, Pallas kernels: 47.7 us -> 49.4 us  [still_shards(): pl.pallas_call(functools.partial(still_kernel, scale=1.0 / math.sqrt(widt...]
    reshape x4 -> x0, local copies, waits for them, and re-layouts: 1.7 us -> none  [the longest x2 0.89 us: still_shards(): queries.reshape(own, DEVS, heads, width).transpose(1, 2, 0, 3)]
where the time goes in v2:
time: 51.2 us; the launch traced here: 51 us
  Pallas kernels  49.4 us (96%)
  local copies, waits for them, and re-layouts  1.55 us (3%)
    pallas_call x1, Pallas kernels, still_shards(): pl.pallas_call(functools.partial(still_kernel, scale=1.0 / math.sqrt(widt...  49.4 us
    unnamed x1, local copies, waits for them, and re-layouts  1.55 us

profile of v2, /device:TPU:0, one launch (start us, length us, event | category | flops | bytes accessed | tf_op | source)
XLA Modules:
  0.0 51.0 jit_solution(2957551032350958182)
XLA Ops:
  0.0 49.4 %still_attention.1 = bf16[8,7168]{1,0:T(8,128)(2,1)} custom-call(s32[3,16]{1,0:T(4,128)} %bitcast.5, s32[16]{0:T(128)} %slots.1, s32[2]{0:T(128)} %lengths.1, bf16[2,4,16,192]{3,2,1,0:T(8,128)(2,1)} %queries_hbm.1, bf16[2,4,576]{2,1,0:T(4,128)(2,1)} %fresh_hbm.1, bf16[16,576,128]{2,1,0:T(8,128)(2,1)} %bitcast.3, bf16[16,576,128]{2,1,0:T(8,128)(2,1)} %bitcast.4, ...), custom_call_target="tpu_custom_call" | custom-call | tf_op jit(solution)/shard_map/still_attention/pallas_call | solution.py:496
  49.4 1.6 %copy.12 = bf16[8,7168]{1,0:T(8,128)(2,1)} copy(bf16[8,7168]{1,0:T(8,128)(2,1)} %still_attention.1) | data formatting | bytes 229376

commit v3 on v2

--- a/solution.py
+++ b/solution.py
@@ -203,6 +203,7 @@
     absorb,
     expand,
     weight,
+    ropes,
     asked,
     lens,
     absorbed,
@@ -220,6 +221,8 @@
     q_recv,
     n_send,
     n_recv,
+    r_send,
+    r_recv,
     a_send,
     a_recv,
     o_send,
@@ -288,10 +291,10 @@
             if part.shape[1] < nope:
                 part = jnp.concatenate([part, jnp.zeros((all_heads, nope - part.shape[1]), jnp.float32)], axis=1)
             ref[pl.ds(r, all_heads, stride=own), :] = part
-    by_head[:, :, 0:nope] = spread[...].astype(jnp.bfloat16).reshape(DEVS, heads * own, nope)
-    by_head[:, :, nope:width] = (
-        spread_rope[:, 0 : width - nope].astype(jnp.bfloat16).reshape(DEVS, heads * own, width - nope)
-    )
+    by_head[...] = spread[...].astype(jnp.bfloat16).reshape(by_head.shape)
+    turned = spread_rope[:, 0 : width - nope].reshape(DEVS, heads * own, width - nope)
+    middle = heads * own // 2
+    ropes[0] = jnp.concatenate([turned[:, :middle], turned[:, middle:]], axis=2).astype(jnp.bfloat16)
     asks = {}
     for step in (3, 2, 1):
         asks[step] = launch(
@@ -303,6 +306,9 @@
         length_rows = jnp.where(request_row == r, lengths[r], length_rows)
     lens[0] = length_rows
     counts = {}
+    rotary = {}
+    for step in (3, 2, 1):
+        rotary[step] = launch(remote(ropes.at[0], ropes.at[step], r_send.at[step], r_recv.at[step], step))
     for step in (3, 2, 1):
         counts[step] = launch(remote(lens.at[0], lens.at[step], n_send.at[step], n_recv.at[step], step))
 
@@ -321,17 +327,26 @@
         piece = jnp.concatenate([a[head * own : (head + 1) * own] for a in asking], axis=0).astype(
             jnp.bfloat16
         )
-        latent = jnp.dot(piece[:, :nope], absorb[head], preferred_element_type=jnp.float32)
-        absorbed[0, pl.ds(head * rows, rows), 0:rank] = latent.astype(jnp.bfloat16)
-        absorbed[0, pl.ds(head * rows, rows), rank:lat] = piece[:, nope:]
+        latent = jnp.dot(piece, absorb[head], preferred_element_type=jnp.float32)
+        absorbed[0, pl.ds(head * rows, rows), :] = latent.astype(jnp.bfloat16)
     shares = {}
-    for step in (1, 3, 2):
-        shares[step] = launch(
-            remote(absorbed.at[0], absorbed.at[step], a_send.at[step], a_recv.at[step], step)
+    for step in (2, 1):
+        for part in range(2):
+            at = pl.ds(part * (span // 2), span // 2)
+            shares[step, part] = launch(
+                remote(absorbed.at[0, at], absorbed.at[step, at], a_send.at[step, part], a_recv.at[step, part], step)
+            )
+
+    def hand_on(part):
+        at = pl.ds(part * (span // 2), span // 2)
+        shares[2, part].wait_recv()
+        shares[3, part] = launch(
+            remote(absorbed.at[2, at], absorbed.at[3, at], a_send.at[3, part], a_recv.at[3, part], 1)
         )
 
     for step in (1, 2, 3):
         counts[step].wait_recv()
+        rotary[step].wait_recv()
     lane = lax.broadcasted_iota(jnp.int32, (rows, block), 1)
     row = lax.broadcasted_iota(jnp.int32, (rows, block), 0)
     row_length = jnp.concatenate([lens[step] for step in range(DEVS)], axis=0)
@@ -357,12 +372,25 @@
         load.wait()
 
     cuts = [(at, min(CHUNK, total_rows - at)) for at in range(0, total_rows, CHUNK)]
-    for step in (0, 1, 3, 2):
-        if step:
-            shares[step].wait_recv()
-        shard = absorbed[step]
+    for step in range(DEVS):
+        if step == 1:
+            hand_on(0)
+        if step == 2:
+            hand_on(1)
+        if step in (1, 3):
+            for part in range(2):
+                shares[step, part].wait_recv()
+        holder = partner(me, step)
+        order = [s ^ step for s in range(DEVS)]
+        turned = []
+        for s in order:
+            packed = ropes[s, holder].astype(jnp.float32)
+            turned.append(jnp.concatenate([packed[:, : width - nope], packed[:, width - nope :]], axis=0))
+        turned = jnp.concatenate(
+            [a[head * own : (head + 1) * own] for head in range(heads) for a in turned], axis=0
+        ).astype(jnp.bfloat16)
+        shard = jnp.concatenate([absorbed[step], turned], axis=1)
         top = jnp.full((span, 1), FAR, jnp.float32)
-        order = [s ^ step for s in range(DEVS)]
         for at, size in cuts:
             piece = jnp.dot(shard, keys[:, pl.ds(at, size)], preferred_element_type=jnp.float32)
             mask = jnp.concatenate(
@@ -492,6 +520,7 @@
     vmem = pl.BlockSpec(memory_space=pltpu.VMEM)
     far = pl.BlockSpec(memory_space=pl.ANY)
     pair = pltpu.SemaphoreType.DMA((DEVS,))
+    halves = pltpu.SemaphoreType.DMA((DEVS, 2))
     bf16 = jnp.bfloat16
     return pl.pallas_call(
         functools.partial(still_kernel, scale=1.0 / math.sqrt(width)),
@@ -502,15 +531,16 @@
             pltpu.VMEM(queries.shape, bf16),
             pltpu.VMEM((own * all_heads, 128), jnp.float32),
             pltpu.VMEM((own * all_heads, 128), jnp.float32),
-            pltpu.VMEM((DEVS, heads * own, width), bf16),
+            pltpu.VMEM((DEVS, heads * own, key_absorb.shape[1]), bf16),
             pltpu.VMEM(new_latents.shape, bf16),
             pltpu.VMEM((lat, total_rows), bf16),
             pltpu.VMEM(key_absorb.shape, bf16),
             pltpu.VMEM(value_expand.shape, bf16),
             pltpu.VMEM(output_weight.shape, bf16),
-            pltpu.VMEM((DEVS, heads * own, width), bf16),
+            pltpu.VMEM((DEVS, DEVS, heads * own // 2, 2 * (width - key_absorb.shape[1])), bf16),
+            pltpu.VMEM((DEVS, heads * own, key_absorb.shape[1]), bf16),
             pltpu.VMEM((DEVS, own, 128), jnp.int32),
-            pltpu.VMEM((DEVS, span, lat), bf16),
+            pltpu.VMEM((DEVS, span, rank), bf16),
             pltpu.VMEM((rows, total_rows), jnp.float32),
             pltpu.VMEM((span, total_rows), jnp.float32),
             pltpu.VMEM((DEVS, span, rank), bf16),
@@ -527,6 +557,8 @@
             pair,
             pair,
             pair,
+            halves,
+            halves,
             pair,
             pair,
             pair,

time: 51.2 us -> 48.7 us (0.951)
  Pallas kernels: 49.4 us -> 46.9 us
    pallas_call x1, Pallas kernels: 49.4 us -> 46.9 us  [still_shards(): pl.pallas_call(functools.partial(still_kernel, scale=1.0 / math.sqrt(widt...]
where the time goes in v3:
time: 48.7 us; the launch traced here: 48.5 us
  Pallas kernels  46.9 us (96%)
  local copies, waits for them, and re-layouts  1.55 us (3%)
    pallas_call x1, Pallas kernels, still_shards(): pl.pallas_call(functools.partial(still_kernel, scale=1.0 / math.sqrt(widt...  46.9 us
    unnamed x1, local copies, waits for them, and re-layouts  1.55 us

profile of v3, /device:TPU:0, one launch (start us, length us, event | category | flops | bytes accessed | tf_op | source)
XLA Modules:
  0.0 48.5 jit_solution(13774489096047802334)
XLA Ops:
  0.0 46.9 %still_attention.1 = bf16[8,7168]{1,0:T(8,128)(2,1)} custom-call(s32[3,16]{1,0:T(4,128)} %bitcast.5, s32[16]{0:T(128)} %slots.1, s32[2]{0:T(128)} %lengths.1, bf16[2,4,16,192]{3,2,1,0:T(8,128)(2,1)} %queries_hbm.1, bf16[2,4,576]{2,1,0:T(4,128)(2,1)} %fresh_hbm.1, bf16[16,576,128]{2,1,0:T(8,128)(2,1)} %bitcast.3, bf16[16,576,128]{2,1,0:T(8,128)(2,1)} %bitcast.4, ...), custom_call_target="tpu_custom_call" | custom-call | tf_op jit(solution)/shard_map/still_attention/pallas_call | solution.py:525
  46.9 1.6 %copy.12 = bf16[8,7168]{1,0:T(8,128)(2,1)} copy(bf16[8,7168]{1,0:T(8,128)(2,1)} %still_attention.1) | data formatting | bytes 229376

commit v4 on v3

--- a/solution.py
+++ b/solution.py
@@ -258,13 +258,11 @@
         for source, count, first in ((prompt_hbm, held, 0), (resident_hbm, homes, held))
         for b in range(count)
     ]
-    for load in loads[:3] + blocks + loads[3:]:
-        load.start()
-
     barrier = pltpu.get_barrier_semaphore()
     for step in range(1, DEVS):
         pl.semaphore_signal(barrier, inc=1, device_id={"dev": partner(me, step)}, device_id_type=MESH)
-    pl.semaphore_wait(barrier, DEVS - 1)
+    for load in loads[:3]:
+        load.start()
 
     def remote(source, target, send, recv, step):
         return pltpu.make_async_remote_copy(
@@ -295,11 +293,14 @@
     turned = spread_rope[:, 0 : width - nope].reshape(DEVS, heads * own, width - nope)
     middle = heads * own // 2
     ropes[0] = jnp.concatenate([turned[:, :middle], turned[:, middle:]], axis=2).astype(jnp.bfloat16)
+    pl.semaphore_wait(barrier, DEVS - 1)
     asks = {}
     for step in (3, 2, 1):
         asks[step] = launch(
             remote(by_head.at[partner(me, step)], asked.at[step], q_send.at[step], q_recv.at[step], step)
         )
+    for load in blocks + loads[3:]:
+        load.start()
     request_row = lax.broadcasted_iota(jnp.int32, (own, 128), 0) // steps
     length_rows = jnp.zeros((own, 128), jnp.int32)
     for r in range(requests):
@@ -323,19 +324,20 @@
         asks[step].wait_recv()
     loads[1].wait()
     asking = [asked[step].astype(jnp.float32) for step in range(DEVS)]
+    shares = {}
     for head in range(heads):
         piece = jnp.concatenate([a[head * own : (head + 1) * own] for a in asking], axis=0).astype(
             jnp.bfloat16
         )
         latent = jnp.dot(piece, absorb[head], preferred_element_type=jnp.float32)
         absorbed[0, pl.ds(head * rows, rows), :] = latent.astype(jnp.bfloat16)
-    shares = {}
-    for step in (2, 1):
-        for part in range(2):
+        part = 2 * (head + 1) // heads - 1
+        if 2 * (head + 1) % heads == 0:
             at = pl.ds(part * (span // 2), span // 2)
-            shares[step, part] = launch(
-                remote(absorbed.at[0, at], absorbed.at[step, at], a_send.at[step, part], a_recv.at[step, part], step)
-            )
+            for step in (2, 1):
+                shares[step, part] = launch(
+                    remote(absorbed.at[0, at], absorbed.at[step, at], a_send.at[step, part], a_recv.at[step, part], step)
+                )
 
     def hand_on(part):
         at = pl.ds(part * (span // 2), span // 2)
@@ -515,7 +517,7 @@
     span = heads * rows
     rank = key_absorb.shape[2]
     model = output_weight.shape[1]
-    pieces = 4
+    pieces = 2
     smem = pl.BlockSpec(memory_space=pltpu.SMEM)
     vmem = pl.BlockSpec(memory_space=pltpu.VMEM)
     far = pl.BlockSpec(memory_space=pl.ANY)

time: 48.7 us -> 47 us (0.965)
  Pallas kernels: 46.9 us -> 45.3 us
    pallas_call x1, Pallas kernels: 46.9 us -> 45.3 us  [still_shards(): pl.pallas_call(functools.partial(still_kernel, scale=1.0 / math.sqrt(widt...]
where the time goes in v4:
time: 47 us; the launch traced here: 46.8 us
  Pallas kernels  45.3 us (96%)
  local copies, waits for them, and re-layouts  1.55 us (3%)
    pallas_call x1, Pallas kernels, still_shards(): pl.pallas_call(functools.partial(still_kernel, scale=1.0 / math.sqrt(widt...  45.3 us
    unnamed x1, local copies, waits for them, and re-layouts  1.55 us

profile of v4, /device:TPU:0, one launch (start us, length us, event | category | flops | bytes accessed | tf_op | source)
XLA Modules:
  0.0 46.8 jit_solution(18264591790934396673)
XLA Ops:
  0.0 45.3 %still_attention.1 = bf16[8,7168]{1,0:T(8,128)(2,1)} custom-call(s32[3,16]{1,0:T(4,128)} %bitcast.5, s32[16]{0:T(128)} %slots.1, s32[2]{0:T(128)} %lengths.1, bf16[2,4,16,192]{3,2,1,0:T(8,128)(2,1)} %queries_hbm.1, bf16[2,4,576]{2,1,0:T(4,128)(2,1)} %fresh_hbm.1, bf16[16,576,128]{2,1,0:T(8,128)(2,1)} %bitcast.3, bf16[16,576,128]{2,1,0:T(8,128)(2,1)} %bitcast.4, ...), custom_call_target="tpu_custom_call" | custom-call | tf_op jit(solution)/shard_map/still_attention/pallas_call | solution.py:527
  45.3 1.6 %copy.12 = bf16[8,7168]{1,0:T(8,128)(2,1)} copy(bf16[8,7168]{1,0:T(8,128)(2,1)} %still_attention.1) | data formatting | bytes 229376
